TPU v7x, 32 devices: a whole 2x2x4 slice. The times are simulated.
32 devices in a mesh: groups: 2 (over x), ep: 16 (over z, y, core).
Axes of the slice: x: 2, y: 2, z: 4, core: 2. Of those that a mesh axis runs over, the one named last changes fastest.
Arguments:
- residual: bfloat16 [512, 2048], P(('groups', 'ep')), parts along dimension 0, may hold values from -54 to 54
- norm_gain: bfloat16 [2048], replicated, may hold values from 0.099609375 to 1.8984375
- expert_ids: int32 [512, 8], P(('groups', 'ep')), parts along dimension 0, may hold values from 0 to 15, as said below
- route_weights: float32 [512, 8], P(('groups', 'ep')), parts along dimension 0, may hold values from 0.05 to 1
- w_gate: bfloat16 [16, 2, 2048, 384], P('ep'), may hold values from -0.125 to 0.125
- w_up: bfloat16 [16, 2, 2048, 384], P('ep'), may hold values from -0.125 to 0.125
- w_down: bfloat16 [16, 2, 384, 2048], P('ep'), may hold values from -0.21875 to 0.21875
Outputs:
- layer_out: bfloat16 [512, 2048], P(('groups', 'ep')), parts along dimension 0
There are 2 independent parts, one for each index of `groups`. A program takes and returns all parts, laid end to end along the dimension named above; an argument that names none is the same for every part. Nothing has to cross between parts.
Inputs may be any that keep to these rules, and one draw needn't show every extreme that they name: `expert_ids`: each row names 8 different experts. Among the rows of one device no expert is named by more than 16 rows, and no pair of experts 2 j and 2 j + 1 by more than 16 rows (a row that names both counts once); each bound is reached on some device.
All inputs are finite; a program needn't handle non-finite values.
Results may differ from a plain program's by a relative error of at most 0.004.
Values may be sent and summed in bfloat16 or wider, within the bound.
A program may use at most 64 MiB of HBM per device.

v0:
```python
import jax
import jax.numpy as jnp
from jax import lax
from jax.sharding import PartitionSpec as P

TOP = 8


def swapped(value, axis, distance):
    mask = 2**distance
    pairs = [(source, source ^ mask) for source in range(lax.axis_size(axis))]
    return lax.ppermute(value, axis, pairs)


def half_ffn(inputs, gate_mat, up_mat, down_mat):
    gate_part = jnp.dot(inputs, gate_mat, preferred_element_type=jnp.float32)
    upper = jnp.dot(inputs, up_mat, preferred_element_type=jnp.float32)
    inner = (jax.nn.silu(gate_part) * upper).astype(jnp.bfloat16)
    return jnp.dot(inner, down_mat, preferred_element_type=jnp.float32)


def pair_tables(expert_ids, shares, normed, block_total, slot_total):
    local_rows = normed.shape[0]
    expert_total = 2 * block_total
    block_iota = lax.broadcasted_iota(jnp.int32, (1, 1, block_total), 2)
    block_hits = jnp.any((expert_ids // 2)[:, :, None] == block_iota, axis=1).astype(jnp.int32)
    block_rank = jnp.cumsum(block_hits, axis=0) - 1
    hit_wide = jnp.repeat(block_hits, slot_total, axis=1)
    rank_wide = jnp.repeat(block_rank, slot_total, axis=1)
    slot_place = lax.broadcasted_iota(jnp.int32, (1, block_total * slot_total), 1) % slot_total
    picker = jnp.logical_and(hit_wide > 0, rank_wide == slot_place)
    expert_iota = lax.broadcasted_iota(jnp.int32, (1, 1, expert_total), 2)
    expert_mask = expert_ids[:, :, None] == expert_iota
    share_table = jnp.sum(
        jnp.where(expert_mask, shares[:, :, None], jnp.zeros((), jnp.bfloat16)), axis=1
    )
    share_wide = jnp.repeat(share_table.reshape(local_rows, block_total, 2), slot_total, axis=1)
    slot_weights = jnp.sum(
        jnp.where(picker[:, :, None], share_wide, jnp.zeros((), jnp.bfloat16)), axis=0
    )
    slot_rows = jnp.einsum(
        "rs,rd->sd", picker.astype(jnp.bfloat16), normed, preferred_element_type=jnp.float32
    ).astype(jnp.bfloat16)
    return (picker, slot_rows, slot_weights)


def local(residual, norm_gain, expert_ids, route_weights, w_gate, w_up, w_down):
    local_rows = residual.shape[0]
    model_width = residual.shape[1]
    widened = residual.astype(jnp.float32)
    scaling = lax.rsqrt(jnp.mean(widened * widened, axis=1, keepdims=True) + 1e-06)
    normed = (widened * scaling * norm_gain.astype(jnp.float32)[None, :]).astype(jnp.bfloat16)
    shares = (route_weights / jnp.sum(route_weights, axis=1, keepdims=True)).astype(jnp.bfloat16)
    device_total = lax.axis_size("ep")
    block_total = device_total // 2
    typical = max(1, local_rows * TOP // device_total)

    def weighted_both(arrived, arrived_weights):
        flat_rows = arrived.reshape(-1, arrived.shape[2])
        flat_weights = arrived_weights.reshape(-1, 2).astype(jnp.float32)
        mixed = flat_weights[:, 0:1] * half_ffn(flat_rows, w_gate[0, 0], w_up[0, 0], w_down[0, 0])
        mixed = mixed + flat_weights[:, 1:2] * half_ffn(
            flat_rows, w_gate[0, 1], w_up[0, 1], w_down[0, 1]
        )
        return mixed.reshape(arrived.shape)

    pair_slots = min(local_rows, 4 * typical)
    half_slots = (pair_slots + 1) // 2
    padded_slots = 2 * half_slots
    picker, slot_rows, slot_weights = pair_tables(
        expert_ids, shares, normed, block_total, padded_slots
    )
    outgoing = slot_rows.reshape(device_total, half_slots, model_width)
    weights_out = slot_weights.reshape(device_total, half_slots, 2)
    arrived = lax.all_to_all(outgoing, "ep", split_axis=0, concat_axis=0, tiled=True)
    arrived_weights = lax.all_to_all(weights_out, "ep", split_axis=0, concat_axis=0, tiled=True)
    other_rows, other_weights = swapped((arrived, arrived_weights), "ep", 0)
    mine = weighted_both(arrived, arrived_weights)
    theirs = weighted_both(other_rows, other_weights)
    back = swapped(theirs, "ep", 0)
    answered = mine + back
    returned = lax.all_to_all(answered, "ep", split_axis=0, concat_axis=0, tiled=True)
    pooled = returned.reshape(block_total * padded_slots, model_width)
    combined = jnp.dot(picker.astype(jnp.float32), pooled, precision=lax.Precision.HIGHEST)
    return (widened + combined).astype(jnp.bfloat16)


def solution(mesh):
    placed = (
        P(("groups", "ep"), None),
        P(),
        P(("groups", "ep"), None),
        P(("groups", "ep"), None),
        P("ep", None, None, None),
        P("ep", None, None, None),
        P("ep", None, None, None),
    )
    return jax.shard_map(
        local, mesh=mesh, in_specs=placed, out_specs=P(("groups", "ep"), None), check_vma=False
    )
```

profile of v0, /device:TPU:9, one launch (start us, length us, event | category | flops | bytes accessed | tf_op | source)
XLA Modules:
  0.0 88.5 jit_solution(8988747759882350562)
XLA Ops:
  0.0 0.8 copy.44
  1.0 0.7 convert_element_type.56
  1.7 1.0 %fusion.76 = f32[16]{0:T(128)S(1)} fusion(bf16[16,2048]{1,0:T(8,128)(2,1)} %param.7), kind=kLoop, calls=%fused_computation.72 | loop fusion | flops 98288 | bytes 65600 | tf_op jit(solution)/shard_map/reduce_sum | solution.py:51
  3.0 2.0 %fusion.5 = bf16[16,8,2048]{2,1,0:T(8,128)(2,1)} fusion(bf16[16,2048]{1,0:T(8,128)(2,1)} %param.7, f32[2048]{0:T(1024)S(1)} %convert_element_type.56, f32[16]{0:T(128)S(1)} %add_rsqrt_fusion, pred[16,128]{1,0:T(8,128)(4,1)S(1)} %gt.16, s32[16,128]{1,0:T(8,128)S(1)} %reshape.127, s32[128]{0:T(128)S(1)} %and_select_fusion), kind=kOutput, calls=%fused_computation.10 | convolution fusion | flops 8785920 | bytes 608832 | tf_op jit(solution)/shard_map/rs,rd->sd/dot_general | solution.py:41
  5.0 6.6 %all-to-all-start.1 = ((bf16[16,8,2048]{2,1,0:T(8,128)(2,1)}), bf16[16,8,2048]{2,1,0:T(8,128)(2,1)S(1)}, u32[]{:S(2)}, u32[]{:S(2)}) async-start(bf16[16,8,2048]{2,1,0:T(8,128)(2,1)} %fusion.5), calls=%async_computation.1 | async-start | bytes 1048576 | tf_op jit(solution)/shard_map/all_to_all | solution.py:75
  11.6 0.7 reduce_sum.42
  12.3 0.7 divide_convert_fusion
  13.1 0.1 fusion.103
  13.4 12.3 %all-to-all-done.1 = bf16[16,8,2048]{2,1,0:T(8,128)(2,1)S(1)} async-done(((bf16[16,8,2048]{2,1,0:T(8,128)(2,1)}), bf16[16,8,2048]{2,1,0:T(8,128)(2,1)S(1)}, u32[]{:S(2)}, u32[]{:S(2)}) %all-to-all-start.1) | async-done | bytes 524320 | tf_op jit(solution)/shard_map/all_to_all | solution.py:75
  26.1 9.2 %all_to_all.15 = bf16[16,8,2]{1,2,0:T(2,128)(2,1)S(1)} all-to-all(bf16[16,8,2]{1,2,0:T(2,128)(2,1)S(1)} %copy.54), channel_id=1, replica_groups=mesh['groups'=2,'ep'=16] {'ep'}, dimensions={0} | all-to-all | bytes 1024 | tf_op jit(solution)/shard_map/all_to_all | solution.py:76
  35.4 0.7 collective-permute-start
  36.2 0.7 collective-permute-done
  37.0 1.8 %fusion.19 = f32[128,384]{1,0:T(8,128)S(1)} fusion(bf16[1,2,2048,384]{3,2,1,0:T(8,128)(2,1)} %param.12, bf16[16,8,2048]{2,1,0:T(8,128)(2,1)S(1)} %collective-permute-done.1), kind=kOutput, calls=%fused_computation.25 | convolution fusion | flops 201326592 | bytes 2293760 | tf_op jit(solution)/shard_map/dot_general | solution.py:17
  38.9 1.8 %fusion.9 = f32[128,384]{1,0:T(8,128)S(1)} fusion(bf16[1,2,2048,384]{3,2,1,0:T(8,128)(2,1)} %param.12, bf16[16,8,2048]{2,1,0:T(8,128)(2,1)S(1)} %collective-permute-done.1), kind=kOutput, calls=%fused_computation.15 | convolution fusion | flops 201326592 | bytes 2293760 | tf_op jit(solution)/shard_map/dot_general | solution.py:17
  40.7 2.7 %convolution_multiply_fusion.1 = f32[128,2048]{1,0:T(8,128)S(1)} fusion(bf16[1,2,384,2048]{3,2,1,0:T(8,128)(2,1)} %param.13, f32[128]{0:T(128)S(1)} %get-tuple-element.10, f32[128,384]{1,0:T(8,128)S(1)} %fusion.19, bf16[1,2,2048,384]{3,2,1,0:T(8,128)(2,1)} %param.11, bf16[16,8,2048]{2,1,0:T(8,128)(2,1)S(1)} %collective-permute-done.1), kind=kOutput, calls=%fused_computation.3 | convolution fusion | flops 403210240 | bytes 4915712 | tf_op jit(solution)/shard_map/dot_general | solution.py:19
  43.5 3.7 %fusion.1 = f32[16,8,2048]{2,1,0:T(8,128)} fusion(f32[128,2048]{1,0:T(8,128)S(1)} %convolution_multiply_fusion.1, bf16[1,2,384,2048]{3,2,1,0:T(8,128)(2,1)} %param.13, f32[128]{0:T(128)S(1)} %get-tuple-element.9, f32[128,384]{1,0:T(8,128)S(1)} %fusion.9, bf16[1,2,2048,384]{3,2,1,0:T(8,128)(2,1)} %param.11, bf16[16,8,2048]{2,1,0:T(8,128)(2,1)S(1)} %collective-permute-done.1), kind=kOutput, calls=%fused_computation.2 | convolution fusion | flops 403472384 | bytes 5964288 | tf_op jit(solution)/shard_map/dot_general | solution.py:19
  47.2 0.3 collective-permute-start.2
  47.6 1.8 %fusion.25 = f32[128,384]{1,0:T(8,128)S(1)} fusion(bf16[1,2,2048,384]{3,2,1,0:T(8,128)(2,1)} %param.11, bf16[16,8,2048]{2,1,0:T(8,128)(2,1)S(1)} %all-to-all-done.1), kind=kOutput, calls=%fused_computation.31 | convolution fusion | flops 201326592 | bytes 2293760 | tf_op jit(solution)/shard_map/dot_general | solution.py:16
  49.4 1.8 %fusion.15 = f32[128,384]{1,0:T(8,128)S(1)} fusion(bf16[1,2,2048,384]{3,2,1,0:T(8,128)(2,1)} %param.11, bf16[16,8,2048]{2,1,0:T(8,128)(2,1)S(1)} %all-to-all-done.1), kind=kOutput, calls=%fused_computation.21 | convolution fusion | flops 201326592 | bytes 2293760 | tf_op jit(solution)/shard_map/dot_general | solution.py:16
  51.3 2.7 %convolution_multiply_fusion.3 = f32[128,2048]{1,0:T(8,128)S(1)} fusion(bf16[1,2,384,2048]{3,2,1,0:T(8,128)(2,1)} %param.13, bf16[1,2,2048,384]{3,2,1,0:T(8,128)(2,1)} %param.12, bf16[16,8,2048]{2,1,0:T(8,128)(2,1)S(1)} %all-to-all-done.1, f32[128]{0:T(128)S(1)} %get-tuple-element.8, f32[128,384]{1,0:T(8,128)S(1)} %fusion.25), kind=kOutput, calls=%fused_computation.7 | convolution fusion | flops 403210240 | bytes 4915712 | tf_op jit(solution)/shard_map/dot_general | solution.py:19
  54.0 3.8 %fusion.4 = f32[16,8,2048]{2,1,0:T(8,128)} fusion(f32[16,8,2048]{2,1,0:T(8,128)S(1)} %collective-permute-done.2, f32[128,2048]{1,0:T(8,128)S(1)} %convolution_multiply_fusion.3, bf16[1,2,384,2048]{3,2,1,0:T(8,128)(2,1)} %param.13, bf16[1,2,2048,384]{3,2,1,0:T(8,128)(2,1)} %param.12, bf16[16,8,2048]{2,1,0:T(8,128)(2,1)S(1)} %all-to-all-done.1, ...), kind=kOutput, calls=%fused_computation.8 | convolution fusion | flops 403734528 | bytes 7012864 | tf_op jit(solution)/shard_map/dot_general | solution.py:19
  57.8 4.8 %all-to-all-start.2 = ((f32[16,8,2048]{2,1,0:T(8,128)}), f32[16,8,2048]{2,1,0:T(8,128)S(1)}, u32[]{:S(2)}, u32[]{:S(2)}) async-start(f32[16,8,2048]{2,1,0:T(8,128)} %fusion.4), calls=%async_computation.2 | async-start | bytes 2097152 | tf_op jit(solution)/shard_map/all_to_all | solution.py:82
  62.7 24.8 %all-to-all-done.2 = f32[16,8,2048]{2,1,0:T(8,128)S(1)} async-done(((f32[16,8,2048]{2,1,0:T(8,128)}), f32[16,8,2048]{2,1,0:T(8,128)S(1)}, u32[]{:S(2)}, u32[]{:S(2)}) %all-to-all-start.2) | async-done | bytes 1048608 | tf_op jit(solution)/shard_map/all_to_all | solution.py:82
  87.5 1.1 %fusion.6 = bf16[16,2048]{1,0:T(8,128)(2,1)} fusion(pred[16,128]{1,0:T(8,128)(4,1)S(1)} %and.45, f32[16,8,2048]{2,1,0:T(8,128)S(1)} %all-to-all-done.2, bf16[16,2048]{1,0:T(8,128)(2,1)S(1)} %copy-done), kind=kOutput, calls=%fused_computation.12 | convolution fusion | flops 50429952 | bytes 1181696 | tf_op jit(solution)/shard_map/dot_general | solution.py:84
  (34 shorter events, 1.7 us)
Async XLA Ops:
  5.0 20.8 %all-to-all-start.1 = ((bf16[16,8,2048]{2,1,0:T(8,128)(2,1)}), bf16[16,8,2048]{2,1,0:T(8,128)(2,1)S(1)}, u32[]{:S(2)}, u32[]{:S(2)}) async-start(bf16[16,8,2048]{2,1,0:T(8,128)(2,1)} %fusion.5), calls=%async_computation.1 | async-start | bytes 1048576 | tf_op jit(solution)/shard_map/all_to_all | solution.py:75
  25.8 11.3 %collective-permute-start.1 = (bf16[16,8,2048]{2,1,0:T(8,128)(2,1)S(1)}, bf16[16,8,2048]{2,1,0:T(8,128)(2,1)S(1)}, u32[]{:S(2)}, u32[]{:S(2)}) collective-permute-start(bf16[16,8,2048]{2,1,0:T(8,128)(2,1)S(1)} %all-to-all-done.1), channel_id=1, source_target_pairs={{0,1},{1,0},{2,3},{3,2},{4,5},{5,4},{6,7},{7,6},{8,9},{9,8},{10,11... | collective-permute-start | bytes 1572872 | tf_op jit(solution)/shard_map/ppermute | solution.py:12
  35.4 1.5 %collective-permute-start = (bf16[16,8,2]{0,1,2:T(8,128)(2,1)S(1)}, bf16[16,8,2]{0,1,2:T(8,128)(2,1)S(1)}, u32[]{:S(2)}, u32[]{:S(2)}) collective-permute-start(bf16[16,8,2]{0,1,2:T(8,128)(2,1)S(1)} %copy.55), channel_id=1, source_target_pairs={{0,1},{1,0},{2,3},{3,2},{4,5},{5,4},{6,7},{7,6},{8,9},{9,8},{10,11... | collective-permute-start | bytes 1544 | tf_op jit(solution)/shard_map/ppermute | solution.py:12
  47.2 6.8 %collective-permute-start.2 = (f32[16,8,2048]{2,1,0:T(8,128)}, f32[16,8,2048]{2,1,0:T(8,128)S(1)}, u32[]{:S(2)}, u32[]{:S(2)}) collective-permute-start(f32[16,8,2048]{2,1,0:T(8,128)} %fusion.1), channel_id=1, source_target_pairs={{0,1},{1,0},{2,3},{3,2},{4,5},{5,4},{6,7},{7,6},{8,9},{9,8},{10,11... | collective-permute-start | bytes 3145736 | tf_op jit(solution)/shard_map/ppermute | solution.py:12
  54.0 33.5 %copy-start = (bf16[16,2048]{1,0:T(8,128)(2,1)S(1)}, bf16[16,2048]{1,0:T(8,128)(2,1)}, u32[]{:S(2)}) copy-start(bf16[16,2048]{1,0:T(8,128)(2,1)} %param.7) | copy-start | bytes 196612
  57.8 29.7 %all-to-all-start.2 = ((f32[16,8,2048]{2,1,0:T(8,128)}), f32[16,8,2048]{2,1,0:T(8,128)S(1)}, u32[]{:S(2)}, u32[]{:S(2)}) async-start(f32[16,8,2048]{2,1,0:T(8,128)} %fusion.4), calls=%async_computation.2 | async-start | bytes 2097152 | tf_op jit(solution)/shard_map/all_to_all | solution.py:82
where the time goes:
time: 89.2 us; the launch traced here: 88.5 us
  waiting for transfers between devices  37.8 us (42%)
  matrix products  23.4 us (26%)
  starting transfers between devices  12.4 us (14%)
  blocking collectives  9.21 us (10%)
  other arithmetic  3.47 us (4%)
  local copies, waits for them, and re-layouts  2.15 us (2%)
    all_to_all x1, waiting for transfers between devices, local(): lax.all_to_all(answered, 'ep', split_axis=0, concat_axis=0, tiled=True)  24.8 us
    dot_general x4, matrix products, half_ffn(): return jnp.dot(inner, down_mat, preferred_element_type=jnp.float32)  13 us
    all_to_all x1, waiting for transfers between devices, local(): lax.all_to_all(outgoing, 'ep', split_axis=0, concat_axis=0, tiled=True)  12.3 us
    all_to_all x1, blocking collectives, local(): lax.all_to_all(weights_out, 'ep', split_axis=0, concat_axis=0, tiled=True)  9.21 us
    all_to_all x1, starting transfers between devices, local(): lax.all_to_all(outgoing, 'ep', split_axis=0, concat_axis=0, tiled=True)  6.61 us
    all_to_all x1, starting transfers between devices, local(): lax.all_to_all(answered, 'ep', split_axis=0, concat_axis=0, tiled=True)  4.79 us
    dot_general x2, matrix products, half_ffn(): upper = jnp.dot(inputs, up_mat, preferred_element_type=jnp.float32)  3.68 us
    dot_general x2, matrix products, half_ffn(): gate_part = jnp.dot(inputs, gate_mat, preferred_element_type=jnp.float32)  3.68 us
  transfers between devices with their start and end apart: 5, of which 3 were waited for; matrix products, arithmetic and copies ran while one was open for 10% of the time, Pallas kernels for 0%

commit v1 on v0

--- a/solution.py
+++ b/solution.py
@@ -1,6 +1,10 @@
+import functools
+
 import jax
 import jax.numpy as jnp
 from jax import lax
+from jax.experimental import pallas as pl
+from jax.experimental.pallas import tpu as pltpu
 from jax.sharding import PartitionSpec as P
 
 TOP = 8
@@ -44,16 +48,298 @@
     return (picker, slot_rows, slot_weights)
 
 
+LANES = 128
+
+
+def mixture_kernel(
+    depth,
+    residual_ref,
+    gain_ref,
+    ids_ref,
+    weights_ref,
+    gate_hbm,
+    up_hbm,
+    down_hbm,
+    out_ref,
+    first_mats,
+    down_mats,
+    rows,
+    kept,
+    core_out,
+    core_in,
+    y_out,
+    y_in,
+    z_out,
+    z_in,
+    weight_sems,
+    rows_recv,
+    rows_z_send,
+    rows_y_send,
+    rows_core_send,
+    core_send,
+    core_recv,
+    y_send,
+    y_recv,
+    z_send,
+    z_recv,
+):
+    place = lax.axis_index("ep")
+    core = place % 2
+    chip = place // 2
+    y_at = chip % 2
+    z_at = chip // 2
+    mate = place + 1 - 2 * core
+    y_peer = place + 2 - 4 * y_at
+
+    def z_peer(step):
+        return ((z_at + step) % depth) * 4 + y_at * 2 + core
+
+    local_rows, width = residual_ref.shape
+    half = gate_hbm.shape[3]
+    hidden = 2 * half
+
+    loads = []
+    for member in range(2):
+        for which, source in enumerate((gate_hbm, up_hbm)):
+            loads.append(
+                pltpu.make_async_copy(
+                    source.at[0, member],
+                    first_mats.at[:, pl.ds(which * hidden + member * half, half)],
+                    weight_sems.at[2 * member + which],
+                )
+            )
+    for member in range(2):
+        loads.append(
+            pltpu.make_async_copy(
+                down_hbm.at[0, member],
+                down_mats.at[pl.ds(member * half, half), :],
+                weight_sems.at[4 + member],
+            )
+        )
+    for load in loads:
+        load.start()
+
+    barrier = pltpu.get_barrier_semaphore()
+    for peer in [mate, y_peer] + [z_peer(step) for step in range(1, depth)]:
+        pl.semaphore_signal(
+            barrier, inc=1, device_id={"ep": peer}, device_id_type=pl.DeviceIdType.MESH
+        )
+
+    widened = residual_ref[...].astype(jnp.float32)
+    scaling = lax.rsqrt(jnp.mean(widened * widened, axis=1, keepdims=True) + 1e-06)
+    gain = gain_ref[...].astype(jnp.float32)
+    rows[0, 0, 0, :, 0:width] = (widened * scaling * gain).astype(jnp.bfloat16)
+    route = weights_ref[...]
+    shares = (route / jnp.sum(route, axis=1, keepdims=True)).astype(jnp.bfloat16).astype(jnp.float32)
+    ids = ids_ref[...]
+    lane = lax.broadcasted_iota(jnp.int32, (local_rows, LANES), 1)
+    table = jnp.zeros((local_rows, LANES), jnp.float32)
+    for choice in range(ids.shape[1]):
+        table = table + jnp.where(
+            ids[:, choice : choice + 1] == lane, shares[:, choice : choice + 1], 0.0
+        )
+    rows[0, 0, 0, :, width : width + LANES] = table.astype(jnp.bfloat16)
+
+    pl.semaphore_wait(barrier, depth + 1)
+
+    started = []
+
+    def send(source, target, send_sem, recv_sem, peer):
+        copy = pltpu.make_async_remote_copy(
+            src_ref=source,
+            dst_ref=target,
+            send_sem=send_sem,
+            recv_sem=recv_sem,
+            device_id={"ep": peer},
+            device_id_type=pl.DeviceIdType.MESH,
+        )
+        copy.start()
+        started.append(copy)
+        return copy
+
+    def arrived(step, dy, dc):
+        slot = rows.at[step, dy, dc]
+        pltpu.make_async_copy(slot, slot, rows_recv.at[step, dy, dc]).wait()
+
+    def landed(buffer, sem):
+        pltpu.make_async_copy(buffer, buffer, sem).wait()
+
+    def rows_to_z(step):
+        send(
+            rows.at[0, 0, 0],
+            rows.at[step, 0, 0],
+            rows_z_send.at[step],
+            rows_recv.at[step, 0, 0],
+            z_peer(step),
+        )
+
+    def rows_to_y(step):
+        send(
+            rows.at[step, 0, 0],
+            rows.at[step, 1, 0],
+            rows_y_send.at[step],
+            rows_recv.at[step, 1, 0],
+            y_peer,
+        )
+
+    def rows_to_mate(step, dy):
+        send(
+            rows.at[step, dy, 0],
+            rows.at[step, dy, 1],
+            rows_core_send.at[step, dy],
+            rows_recv.at[step, dy, 1],
+            mate,
+        )
+
+    def from_z(step):
+        arrived(step, 0, 0)
+        rows_to_y(step)
+        rows_to_mate(step, 0)
+
+    def from_y(step):
+        arrived(step, 1, 0)
+        rows_to_mate(step, 1)
+
+    def compute(step):
+        arrived(step, 0, 1)
+        arrived(step, 1, 1)
+        block = rows[step, :, :, :, 0:width].reshape(4 * local_rows, width)
+        shares_here = rows[step, :, :, :, width : width + LANES].reshape(4 * local_rows, LANES)
+        shares_here = shares_here.astype(jnp.float32)
+        lanes = lax.broadcasted_iota(jnp.int32, (4 * local_rows, LANES), 1)
+        both = jnp.dot(block, first_mats[...], preferred_element_type=jnp.float32)
+        parts = []
+        for member in range(2):
+            share = jnp.sum(
+                jnp.where(lanes == 2 * chip + member, shares_here, 0.0), axis=1, keepdims=True
+            )
+            gate_part = both[:, member * half : (member + 1) * half]
+            upper = both[:, hidden + member * half : hidden + (member + 1) * half]
+            inner = (jax.nn.silu(gate_part) * upper).astype(jnp.bfloat16)
+            parts.append((inner.astype(jnp.float32) * share).astype(jnp.bfloat16))
+        inner = jnp.concatenate(parts, axis=1)
+        answer = jnp.dot(inner, down_mats[...], preferred_element_type=jnp.float32)
+        answer = answer.reshape(2, 2, local_rows, width)
+        kept[step] = answer[:, 0]
+        core_out[step] = answer[:, 1].astype(jnp.bfloat16)
+        send(core_out.at[step], core_in.at[step], core_send.at[step], core_recv.at[step], mate)
+
+    def add_core(step):
+        landed(core_in.at[step], core_recv.at[step])
+        y_out[step] = (kept[step, 1] + core_in[step, 1].astype(jnp.float32)).astype(jnp.bfloat16)
+        send(y_out.at[step], y_in.at[step], y_send.at[step], y_recv.at[step], y_peer)
+        kept[step, 0] = kept[step, 0] + core_in[step, 0].astype(jnp.float32)
+
+    def add_y(step):
+        landed(y_in.at[step], y_recv.at[step])
+        total = kept[step, 0] + y_in[step].astype(jnp.float32)
+        if step == 0:
+            kept[0, 0] = total
+        else:
+            z_out[step] = total.astype(jnp.bfloat16)
+            send(
+                z_out.at[step],
+                z_in.at[step],
+                z_send.at[step],
+                z_recv.at[step],
+                z_peer(depth - step),
+            )
+
+    for step in range(1, depth):
+        rows_to_z(step)
+    rows_to_y(0)
+    rows_to_mate(0, 0)
+    from_y(0)
+    if depth > 1:
+        from_z(1)
+    for load in loads:
+        load.wait()
+    for step in range(depth):
+        compute(step)
+        if step + 2 < depth:
+            from_z(step + 2)
+        if step + 1 < depth:
+            from_y(step + 1)
+        if step >= 1:
+            add_core(step - 1)
+        if step >= 2:
+            add_y(step - 2)
+    add_core(depth - 1)
+    if depth > 1:
+        add_y(depth - 2)
+    add_y(depth - 1)
+
+    total = residual_ref[...].astype(jnp.float32) + kept[0, 0]
+    for step in range(1, depth):
+        landed(z_in.at[step], z_recv.at[step])
+        total = total + z_in[step].astype(jnp.float32)
+    out_ref[...] = total.astype(out_ref.dtype)
+    for copy in started:
+        copy.wait_send()
+
+
+def dense_mixture(residual, norm_gain, expert_ids, route_weights, w_gate, w_up, w_down):
+    local_rows, width = residual.shape
+    half = w_gate.shape[3]
+    device_total = lax.axis_size("ep")
+    depth = device_total // 4
+    dma = pltpu.SemaphoreType.DMA
+    bf16 = jnp.bfloat16
+    vmem = pl.BlockSpec(memory_space=pltpu.VMEM)
+    anywhere = pl.BlockSpec(memory_space=pl.ANY)
+    flops = 2 * device_total * local_rows * width * half * 6
+    return pl.pallas_call(
+        functools.partial(mixture_kernel, depth),
+        out_shape=jax.ShapeDtypeStruct(residual.shape, residual.dtype),
+        in_specs=[vmem] * 4 + [anywhere] * 3,
+        out_specs=vmem,
+        scratch_shapes=[
+            pltpu.VMEM((width, 4 * half), bf16),
+            pltpu.VMEM((2 * half, width), bf16),
+            pltpu.VMEM((depth, 2, 2, local_rows, width + LANES), bf16),
+            pltpu.VMEM((depth, 2, local_rows, width), jnp.float32),
+            pltpu.VMEM((depth, 2, local_rows, width), bf16),
+            pltpu.VMEM((depth, 2, local_rows, width), bf16),
+            pltpu.VMEM((depth, local_rows, width), bf16),
+            pltpu.VMEM((depth, local_rows, width), bf16),
+            pltpu.VMEM((depth, local_rows, width), bf16),
+            pltpu.VMEM((depth, local_rows, width), bf16),
+            dma((6,)),
+            dma((depth, 2, 2)),
+            dma((depth,)),
+            dma((depth,)),
+            dma((depth, 2)),
+            dma((depth,)),
+            dma((depth,)),
+            dma((depth,)),
+            dma((depth,)),
+            dma((depth,)),
+            dma((depth,)),
+        ],
+        compiler_params=pltpu.CompilerParams(
+            collective_id=0, has_side_effects=True, vmem_limit_bytes=62 * 2**20
+        ),
+        cost_estimate=pl.CostEstimate(
+            flops=flops, bytes_accessed=12 * width * half, transcendentals=0
+        ),
+    )(residual, norm_gain[None, :], expert_ids, route_weights, w_gate, w_up, w_down)
+
+
 def local(residual, norm_gain, expert_ids, route_weights, w_gate, w_up, w_down):
     local_rows = residual.shape[0]
     model_width = residual.shape[1]
+    device_total = lax.axis_size("ep")
+    block_total = device_total // 2
+    typical = max(1, local_rows * TOP // device_total)
+    pair_slots = min(local_rows, 4 * typical)
+    if pair_slots == local_rows and device_total % 4 == 0 and device_total <= LANES:
+        return dense_mixture(
+            residual, norm_gain, expert_ids, route_weights, w_gate, w_up, w_down
+        )
     widened = residual.astype(jnp.float32)
     scaling = lax.rsqrt(jnp.mean(widened * widened, axis=1, keepdims=True) + 1e-06)
     normed = (widened * scaling * norm_gain.astype(jnp.float32)[None, :]).astype(jnp.bfloat16)
     shares = (route_weights / jnp.sum(route_weights, axis=1, keepdims=True)).astype(jnp.bfloat16)
-    device_total = lax.axis_size("ep")
-    block_total = device_total // 2
-    typical = max(1, local_rows * TOP // device_total)
 
     def weighted_both(arrived, arrived_weights):
         flat_rows = arrived.reshape(-1, arrived.shape[2])
@@ -64,7 +350,6 @@
         )
         return mixed.reshape(arrived.shape)
 
-    pair_slots = min(local_rows, 4 * typical)
     half_slots = (pair_slots + 1) // 2
     padded_slots = 2 * half_slots
     picker, slot_rows, slot_weights = pair_tables(

time: 89.2 us -> 39.7 us (0.45)
  the two profiles are of different devices: /device:TPU:9 before, /device:TPU:0 now
where the time goes in v1:
time: 39.7 us; the launch traced here: 39.4 us
  Pallas kernels  33.9 us (85%)
  local copies, waits for them, and re-layouts  5.47 us (14%)
    pallas_call x1, Pallas kernels, dense_mixture(): pl.pallas_call(functools.partial(mixture_kernel, depth), out_shape=jax.Sh...  33.9 us
    unnamed x3, local copies, waits for them, and re-layouts  4.18 us
    broadcast_in_dim x1, local copies, waits for them, and re-layouts, dense_mixture(): norm_gain[None, :]  1.29 us

profile of v1, /device:TPU:0, one launch (start us, length us, event | category | flops | bytes accessed | tf_op | source)
XLA Modules:
  0.0 39.4 jit_solution(3533666116810941672)
XLA Ops:
  0.0 1.3 %broadcast_in_dim.3.gain_ref = bf16[1,2048]{1,0:T(2,128)(2,1)} reshape(bf16[2048]{0:T(1024)(128)(2,1)} %param.8) | data formatting | bytes 8192 | tf_op jit(solution)/shard_map/broadcast_in_dim | solution.py:325
  1.3 1.3 %copy.8.ids_ref = s32[16,8]{1,0:T(8,128)} copy(s32[16,8]{0,1:T(8,128)} %param.9) | data formatting | bytes 1024 | tf_op args[2]
  2.6 1.4 %copy.9.weights_ref = f32[16,8]{1,0:T(8,128)} copy(f32[16,8]{0,1:T(8,128)} %param.10) | data formatting | bytes 1024 | tf_op args[3]
  4.0 33.9 %shard_map.73 = bf16[16,2048]{1,0:T(8,128)(2,1)} custom-call(bf16[16,2048]{1,0:T(8,128)(2,1)} %residual_ref.1, bf16[1,2048]{1,0:T(2,128)(2,1)} %broadcast_in_dim.3.gain_ref, s32[16,8]{1,0:T(8,128)} %copy.8.ids_ref, f32[16,8]{1,0:T(8,128)} %copy.9.weights_ref, bf16[1,2,2048,384]{3,2,1,0:T(8,128)(2,1)} %gate_hbm.1, bf16[1,2,2048,384]{3,2,1,0:T(8,128)(2,1)} %up_hbm.1, ...), custom_call_target="tpu_custom_call" | custom-call | flops 2415919104 | bytes 9437184 | tf_op jit(solution)/shard_map/pallas_call | solution.py:291
  37.9 1.5 %copy.11 = bf16[16,2048]{1,0:T(8,128)(2,1)} copy(bf16[16,2048]{1,0:T(8,128)(2,1)} %shard_map.73) | data formatting | bytes 131072

commit v2 on v1

--- a/solution.py
+++ b/solution.py
@@ -53,17 +53,24 @@
 
 def mixture_kernel(
     depth,
+    groups,
+    parts,
+    residual_hbm,
+    gain_hbm,
+    ids_hbm,
+    weights_hbm,
+    gate_hbm,
+    up_hbm,
+    down_hbm,
+    out_ref,
     residual_ref,
     gain_ref,
     ids_ref,
     weights_ref,
-    gate_hbm,
-    up_hbm,
-    down_hbm,
-    out_ref,
     first_mats,
     down_mats,
     rows,
+    inner_ref,
     kept,
     core_out,
     core_in,
@@ -71,6 +78,7 @@
     y_in,
     z_out,
     z_in,
+    small_sems,
     weight_sems,
     rows_recv,
     rows_z_send,
@@ -95,8 +103,28 @@
         return ((z_at + step) % depth) * 4 + y_at * 2 + core
 
     local_rows, width = residual_ref.shape
+    part_width = width // parts
     half = gate_hbm.shape[3]
     hidden = 2 * half
+
+    smalls = []
+    for which, (source, target) in enumerate(
+        (
+            (residual_hbm, residual_ref),
+            (gain_hbm, gain_ref),
+            (ids_hbm, ids_ref),
+            (weights_hbm, weights_ref),
+        )
+    ):
+        smalls.append(pltpu.make_async_copy(source, target, small_sems.at[which]))
+    for load in smalls:
+        load.start()
+
+    barrier = pltpu.get_barrier_semaphore()
+    for peer in [mate, y_peer] + [z_peer(step) for step in range(1, depth)]:
+        pl.semaphore_signal(
+            barrier, inc=1, device_id={"ep": peer}, device_id_type=pl.DeviceIdType.MESH
+        )
 
     loads = []
     for member in range(2):
@@ -116,29 +144,36 @@
                 weight_sems.at[4 + member],
             )
         )
+    for load in smalls:
+        load.wait()
     for load in loads:
         load.start()
 
-    barrier = pltpu.get_barrier_semaphore()
-    for peer in [mate, y_peer] + [z_peer(step) for step in range(1, depth)]:
-        pl.semaphore_signal(
-            barrier, inc=1, device_id={"ep": peer}, device_id_type=pl.DeviceIdType.MESH
-        )
-
     widened = residual_ref[...].astype(jnp.float32)
     scaling = lax.rsqrt(jnp.mean(widened * widened, axis=1, keepdims=True) + 1e-06)
-    gain = gain_ref[...].astype(jnp.float32)
-    rows[0, 0, 0, :, 0:width] = (widened * scaling * gain).astype(jnp.bfloat16)
+    for block in range(width // LANES):
+        columns = slice(block * LANES, (block + 1) * LANES)
+        gain = gain_ref[block : block + 1, :].astype(jnp.float32)
+        rows[0, 0, 0, :, columns] = (widened[:, columns] * scaling * gain).astype(jnp.bfloat16)
     route = weights_ref[...]
-    shares = (route / jnp.sum(route, axis=1, keepdims=True)).astype(jnp.bfloat16).astype(jnp.float32)
+    shares = (route / jnp.sum(route, axis=0, keepdims=True)).astype(jnp.bfloat16).astype(jnp.float32)
     ids = ids_ref[...]
-    lane = lax.broadcasted_iota(jnp.int32, (local_rows, LANES), 1)
-    table = jnp.zeros((local_rows, LANES), jnp.float32)
-    for choice in range(ids.shape[1]):
+    expert = lax.broadcasted_iota(jnp.int32, (LANES, local_rows), 0)
+    table = jnp.zeros((LANES, local_rows), jnp.float32)
+    for choice in range(ids.shape[0]):
         table = table + jnp.where(
-            ids[:, choice : choice + 1] == lane, shares[:, choice : choice + 1], 0.0
-        )
-    rows[0, 0, 0, :, width : width + LANES] = table.astype(jnp.bfloat16)
+            ids[choice : choice + 1, :] == expert, shares[choice : choice + 1, :], 0.0
+        )
+    same = lax.broadcasted_iota(jnp.int32, (local_rows, local_rows), 0) == (
+        lax.broadcasted_iota(jnp.int32, (local_rows, local_rows), 1)
+    )
+    turned = lax.dot_general(
+        same.astype(jnp.float32).astype(jnp.bfloat16),
+        table.astype(jnp.bfloat16),
+        (((1,), (1,)), ((), ())),
+        preferred_element_type=jnp.float32,
+    )
+    rows[0, 0, 0, :, width : width + LANES] = turned.astype(jnp.bfloat16)
 
     pl.semaphore_wait(barrier, depth + 1)
 
@@ -155,14 +190,12 @@
         )
         copy.start()
         started.append(copy)
-        return copy
-
-    def arrived(step, dy, dc):
-        slot = rows.at[step, dy, dc]
-        pltpu.make_async_copy(slot, slot, rows_recv.at[step, dy, dc]).wait()
 
     def landed(buffer, sem):
         pltpu.make_async_copy(buffer, buffer, sem).wait()
+
+    def arrived(step, dy, dc):
+        landed(rows.at[step, dy, dc], rows_recv.at[step, dy, dc])
 
     def rows_to_z(step):
         send(
@@ -192,23 +225,27 @@
         )
 
     def from_z(step):
-        arrived(step, 0, 0)
-        rows_to_y(step)
-        rows_to_mate(step, 0)
+        if 0 < step < depth:
+            arrived(step, 0, 0)
+            rows_to_y(step)
+            rows_to_mate(step, 0)
 
     def from_y(step):
-        arrived(step, 1, 0)
-        rows_to_mate(step, 1)
-
-    def compute(step):
-        arrived(step, 0, 1)
-        arrived(step, 1, 1)
-        block = rows[step, :, :, :, 0:width].reshape(4 * local_rows, width)
-        shares_here = rows[step, :, :, :, width : width + LANES].reshape(4 * local_rows, LANES)
-        shares_here = shares_here.astype(jnp.float32)
-        lanes = lax.broadcasted_iota(jnp.int32, (4 * local_rows, LANES), 1)
+        if step < depth:
+            arrived(step, 1, 0)
+            rows_to_mate(step, 1)
+
+    def first(group):
+        begin, count = groups[group]
+        for step in range(begin, begin + count):
+            arrived(step, 0, 1)
+            arrived(step, 1, 1)
+        total_rows = count * 4 * local_rows
+        block = rows[begin : begin + count, :, :, :, 0:width].reshape(total_rows, width)
+        shares_here = rows[begin : begin + count, :, :, :, width : width + LANES]
+        shares_here = shares_here.reshape(total_rows, LANES).astype(jnp.float32)
+        lanes = lax.broadcasted_iota(jnp.int32, (total_rows, LANES), 1)
         both = jnp.dot(block, first_mats[...], preferred_element_type=jnp.float32)
-        parts = []
         for member in range(2):
             share = jnp.sum(
                 jnp.where(lanes == 2 * chip + member, shares_here, 0.0), axis=1, keepdims=True
@@ -216,64 +253,97 @@
             gate_part = both[:, member * half : (member + 1) * half]
             upper = both[:, hidden + member * half : hidden + (member + 1) * half]
             inner = (jax.nn.silu(gate_part) * upper).astype(jnp.bfloat16)
-            parts.append((inner.astype(jnp.float32) * share).astype(jnp.bfloat16))
-        inner = jnp.concatenate(parts, axis=1)
-        answer = jnp.dot(inner, down_mats[...], preferred_element_type=jnp.float32)
-        answer = answer.reshape(2, 2, local_rows, width)
-        kept[step] = answer[:, 0]
-        core_out[step] = answer[:, 1].astype(jnp.bfloat16)
-        send(core_out.at[step], core_in.at[step], core_send.at[step], core_recv.at[step], mate)
-
-    def add_core(step):
-        landed(core_in.at[step], core_recv.at[step])
-        y_out[step] = (kept[step, 1] + core_in[step, 1].astype(jnp.float32)).astype(jnp.bfloat16)
-        send(y_out.at[step], y_in.at[step], y_send.at[step], y_recv.at[step], y_peer)
-        kept[step, 0] = kept[step, 0] + core_in[step, 0].astype(jnp.float32)
-
-    def add_y(step):
-        landed(y_in.at[step], y_recv.at[step])
-        total = kept[step, 0] + y_in[step].astype(jnp.float32)
-        if step == 0:
-            kept[0, 0] = total
-        else:
-            z_out[step] = total.astype(jnp.bfloat16)
+            inner_ref[0:total_rows, member * half : (member + 1) * half] = (
+                inner.astype(jnp.float32) * share
+            ).astype(jnp.bfloat16)
+
+    def down(group):
+        begin, count = groups[group]
+        steps = pl.ds(begin, count)
+        total_rows = count * 4 * local_rows
+        for part in range(parts):
+            answer = jnp.dot(
+                inner_ref[0:total_rows, :],
+                down_mats[:, part * part_width : (part + 1) * part_width],
+                preferred_element_type=jnp.float32,
+            ).reshape(count, 2, 2, local_rows, part_width)
+            core_out[part, begin : begin + count] = answer[:, :, 1].astype(jnp.bfloat16)
             send(
-                z_out.at[step],
-                z_in.at[step],
-                z_send.at[step],
-                z_recv.at[step],
-                z_peer(depth - step),
-            )
+                core_out.at[part, steps],
+                core_in.at[part, steps],
+                core_send.at[group, part],
+                core_recv.at[group, part],
+                mate,
+            )
+            kept[part, begin : begin + count] = answer[:, :, 0]
+
+    def add_core(group):
+        begin, count = groups[group]
+        steps = pl.ds(begin, count)
+        end = begin + count
+        for part in range(parts):
+            landed(core_in.at[part, steps], core_recv.at[group, part])
+            y_out[part, begin:end] = (
+                kept[part, begin:end, 1] + core_in[part, begin:end, 1].astype(jnp.float32)
+            ).astype(jnp.bfloat16)
+            send(
+                y_out.at[part, steps],
+                y_in.at[part, steps],
+                y_send.at[group, part],
+                y_recv.at[group, part],
+                y_peer,
+            )
+            kept[part, begin:end, 0] = (
+                kept[part, begin:end, 0] + core_in[part, begin:end, 0].astype(jnp.float32)
+            )
+
+    def add_y(group):
+        begin, count = groups[group]
+        for part in range(parts):
+            landed(y_in.at[part, pl.ds(begin, count)], y_recv.at[group, part])
+            for step in range(begin, begin + count):
+                total = kept[part, step, 0] + y_in[part, step].astype(jnp.float32)
+                if step == 0:
+                    kept[part, 0, 0] = total
+                else:
+                    z_out[part, step] = total.astype(jnp.bfloat16)
+                    send(
+                        z_out.at[part, step],
+                        z_in.at[part, step],
+                        z_send.at[step, part],
+                        z_recv.at[step, part],
+                        z_peer(depth - step),
+                    )
 
     for step in range(1, depth):
         rows_to_z(step)
     rows_to_y(0)
     rows_to_mate(0, 0)
     from_y(0)
-    if depth > 1:
-        from_z(1)
+    from_z(1)
+    from_z(2)
+    from_y(1)
     for load in loads:
         load.wait()
-    for step in range(depth):
-        compute(step)
-        if step + 2 < depth:
-            from_z(step + 2)
-        if step + 1 < depth:
-            from_y(step + 1)
-        if step >= 1:
-            add_core(step - 1)
-        if step >= 2:
-            add_y(step - 2)
-    add_core(depth - 1)
-    if depth > 1:
-        add_y(depth - 2)
-    add_y(depth - 1)
-
-    total = residual_ref[...].astype(jnp.float32) + kept[0, 0]
-    for step in range(1, depth):
-        landed(z_in.at[step], z_recv.at[step])
-        total = total + z_in[step].astype(jnp.float32)
-    out_ref[...] = total.astype(out_ref.dtype)
+    for group, (begin, count) in enumerate(groups):
+        first(group)
+        if group >= 1:
+            add_y(group - 1)
+        from_z(begin + 3)
+        from_y(begin + 2)
+        down(group)
+        add_core(group)
+        from_z(begin + 4)
+        from_y(begin + 3)
+    add_y(len(groups) - 1)
+
+    for part in range(parts):
+        columns = slice(part * part_width, (part + 1) * part_width)
+        total = residual_ref[:, columns].astype(jnp.float32) + kept[part, 0, 0]
+        for step in range(1, depth):
+            landed(z_in.at[part, step], z_recv.at[step, part])
+            total = total + z_in[part, step].astype(jnp.float32)
+        out_ref[:, columns] = total.astype(out_ref.dtype)
     for copy in started:
         copy.wait_send()
 
@@ -281,40 +351,50 @@
 def dense_mixture(residual, norm_gain, expert_ids, route_weights, w_gate, w_up, w_down):
     local_rows, width = residual.shape
     half = w_gate.shape[3]
+    choices = expert_ids.shape[1]
     device_total = lax.axis_size("ep")
     depth = device_total // 4
+    groups = [(begin, min(2, depth - begin)) for begin in range(0, depth, 2)]
+    parts = 4
+    part_width = width // parts
     dma = pltpu.SemaphoreType.DMA
     bf16 = jnp.bfloat16
     vmem = pl.BlockSpec(memory_space=pltpu.VMEM)
     anywhere = pl.BlockSpec(memory_space=pl.ANY)
     flops = 2 * device_total * local_rows * width * half * 6
     return pl.pallas_call(
-        functools.partial(mixture_kernel, depth),
+        functools.partial(mixture_kernel, depth, groups, parts),
         out_shape=jax.ShapeDtypeStruct(residual.shape, residual.dtype),
-        in_specs=[vmem] * 4 + [anywhere] * 3,
+        in_specs=[anywhere] * 7,
         out_specs=vmem,
         scratch_shapes=[
+            pltpu.VMEM((local_rows, width), bf16),
+            pltpu.VMEM((width // LANES, LANES), bf16),
+            pltpu.VMEM((choices, local_rows), jnp.int32),
+            pltpu.VMEM((choices, local_rows), jnp.float32),
             pltpu.VMEM((width, 4 * half), bf16),
             pltpu.VMEM((2 * half, width), bf16),
             pltpu.VMEM((depth, 2, 2, local_rows, width + LANES), bf16),
-            pltpu.VMEM((depth, 2, local_rows, width), jnp.float32),
-            pltpu.VMEM((depth, 2, local_rows, width), bf16),
-            pltpu.VMEM((depth, 2, local_rows, width), bf16),
-            pltpu.VMEM((depth, local_rows, width), bf16),
-            pltpu.VMEM((depth, local_rows, width), bf16),
-            pltpu.VMEM((depth, local_rows, width), bf16),
-            pltpu.VMEM((depth, local_rows, width), bf16),
+            pltpu.VMEM((8 * local_rows, 2 * half), bf16),
+            pltpu.VMEM((parts, depth, 2, local_rows, part_width), jnp.float32),
+            pltpu.VMEM((parts, depth, 2, local_rows, part_width), bf16),
+            pltpu.VMEM((parts, depth, 2, local_rows, part_width), bf16),
+            pltpu.VMEM((parts, depth, local_rows, part_width), bf16),
+            pltpu.VMEM((parts, depth, local_rows, part_width), bf16),
+            pltpu.VMEM((parts, depth, local_rows, part_width), bf16),
+            pltpu.VMEM((parts, depth, local_rows, part_width), bf16),
+            dma((4,)),
             dma((6,)),
             dma((depth, 2, 2)),
             dma((depth,)),
             dma((depth,)),
             dma((depth, 2)),
-            dma((depth,)),
-            dma((depth,)),
-            dma((depth,)),
-            dma((depth,)),
-            dma((depth,)),
-            dma((depth,)),
+            dma((len(groups), parts)),
+            dma((len(groups), parts)),
+            dma((len(groups), parts)),
+            dma((len(groups), parts)),
+            dma((depth, parts)),
+            dma((depth, parts)),
         ],
         compiler_params=pltpu.CompilerParams(
             collective_id=0, has_side_effects=True, vmem_limit_bytes=62 * 2**20
@@ -322,7 +402,15 @@
         cost_estimate=pl.CostEstimate(
             flops=flops, bytes_accessed=12 * width * half, transcendentals=0
         ),
-    )(residual, norm_gain[None, :], expert_ids, route_weights, w_gate, w_up, w_down)
+    )(
+        residual,
+        norm_gain.reshape(width // LANES, LANES),
+        expert_ids.T,
+        route_weights.T,
+        w_gate,
+        w_up,
+        w_down,
+    )
 
 
 def local(residual, norm_gain, expert_ids, route_weights, w_gate, w_up, w_down):

time: 39.7 us -> 36 us (0.907)
  local copies, waits for them, and re-layouts: 5.47 us -> 1.47 us
  Pallas kernels: 33.9 us -> 34.3 us
    unnamed x3 -> x1, local copies, waits for them, and re-layouts: 4.18 us -> 1.47 us
    broadcast_in_dim x1 -> x0, local copies, waits for them, and re-layouts: 1.29 us -> none  [dense_mixture(): norm_gain[None, :]]
where the time goes in v2:
time: 36 us; the launch traced here: 35.8 us
  Pallas kernels  34.3 us (95%)
  local copies, waits for them, and re-layouts  1.47 us (4%)
    pallas_call x1, Pallas kernels, dense_mixture(): pl.pallas_call(functools.partial(mixture_kernel, depth, groups, parts), o...  34.3 us
    unnamed x1, local copies, waits for them, and re-layouts  1.47 us

profile of v2, /device:TPU:0, one launch (start us, length us, event | category | flops | bytes accessed | tf_op | source)
XLA Modules:
  0.0 35.8 jit_solution(1060988010031857748)
XLA Ops:
  0.0 34.3 %shard_map.73 = bf16[16,2048]{1,0:T(8,128)(2,1)} custom-call(bf16[16,2048]{1,0:T(8,128)(2,1)} %residual_hbm.1, bf16[16,128]{1,0:T(8,128)(2,1)} %bitcast.3, s32[8,16]{1,0:T(8,128)} %bitcast.4, f32[8,16]{1,0:T(8,128)} %bitcast.5, bf16[1,2,2048,384]{3,2,1,0:T(8,128)(2,1)} %gate_hbm.1, bf16[1,2,2048,384]{3,2,1,0:T(8,128)(2,1)} %up_hbm.1, ...), custom_call_target="tpu_custom_call" | custom-call | flops 2415919104 | bytes 9437184 | tf_op jit(solution)/shard_map/pallas_call | solution.py:365
  34.3 1.5 %copy.9 = bf16[16,2048]{1,0:T(8,128)(2,1)} copy(bf16[16,2048]{1,0:T(8,128)(2,1)} %shard_map.73) | data formatting | bytes 131072

commit v3 on v2

--- a/solution.py
+++ b/solution.py
@@ -100,7 +100,12 @@
     y_peer = place + 2 - 4 * y_at
 
     def z_peer(step):
-        return ((z_at + step) % depth) * 4 + y_at * 2 + core
+        return ((z_at + step + 1) % depth) * 4 + y_at * 2 + core
+
+    def z_source(step):
+        return ((z_at + depth - step - 1) % depth) * 4 + y_at * 2 + core
+
+    own = depth - 1
 
     local_rows, width = residual_ref.shape
     part_width = width // parts
@@ -119,9 +124,8 @@
         smalls.append(pltpu.make_async_copy(source, target, small_sems.at[which]))
     for load in smalls:
         load.start()
-
     barrier = pltpu.get_barrier_semaphore()
-    for peer in [mate, y_peer] + [z_peer(step) for step in range(1, depth)]:
+    for peer in [mate, y_peer] + [z_peer(step) for step in range(own)]:
         pl.semaphore_signal(
             barrier, inc=1, device_id={"ep": peer}, device_id_type=pl.DeviceIdType.MESH
         )
@@ -144,17 +148,17 @@
                 weight_sems.at[4 + member],
             )
         )
+    for load in loads:
+        load.start()
     for load in smalls:
         load.wait()
-    for load in loads:
-        load.start()
 
     widened = residual_ref[...].astype(jnp.float32)
     scaling = lax.rsqrt(jnp.mean(widened * widened, axis=1, keepdims=True) + 1e-06)
     for block in range(width // LANES):
         columns = slice(block * LANES, (block + 1) * LANES)
         gain = gain_ref[block : block + 1, :].astype(jnp.float32)
-        rows[0, 0, 0, :, columns] = (widened[:, columns] * scaling * gain).astype(jnp.bfloat16)
+        rows[own, 0, 0, :, columns] = (widened[:, columns] * scaling * gain).astype(jnp.bfloat16)
     route = weights_ref[...]
     shares = (route / jnp.sum(route, axis=0, keepdims=True)).astype(jnp.bfloat16).astype(jnp.float32)
     ids = ids_ref[...]
@@ -173,7 +177,7 @@
         (((1,), (1,)), ((), ())),
         preferred_element_type=jnp.float32,
     )
-    rows[0, 0, 0, :, width : width + LANES] = turned.astype(jnp.bfloat16)
+    rows[own, 0, 0, :, width : width + LANES] = turned.astype(jnp.bfloat16)
 
     pl.semaphore_wait(barrier, depth + 1)
 
@@ -199,7 +203,7 @@
 
     def rows_to_z(step):
         send(
-            rows.at[0, 0, 0],
+            rows.at[own, 0, 0],
             rows.at[step, 0, 0],
             rows_z_send.at[step],
             rows_recv.at[step, 0, 0],
@@ -225,15 +229,13 @@
         )
 
     def from_z(step):
-        if 0 < step < depth:
-            arrived(step, 0, 0)
-            rows_to_y(step)
-            rows_to_mate(step, 0)
+        arrived(step, 0, 0)
+        rows_to_y(step)
+        rows_to_mate(step, 0)
 
     def from_y(step):
-        if step < depth:
-            arrived(step, 1, 0)
-            rows_to_mate(step, 1)
+        arrived(step, 1, 0)
+        rows_to_mate(step, 1)
 
     def first(group):
         begin, count = groups[group]
@@ -303,8 +305,8 @@
             landed(y_in.at[part, pl.ds(begin, count)], y_recv.at[group, part])
             for step in range(begin, begin + count):
                 total = kept[part, step, 0] + y_in[part, step].astype(jnp.float32)
-                if step == 0:
-                    kept[part, 0, 0] = total
+                if step == own:
+                    kept[part, own, 0] = total
                 else:
                     z_out[part, step] = total.astype(jnp.bfloat16)
                     send(
@@ -312,35 +314,37 @@
                         z_in.at[part, step],
                         z_send.at[step, part],
                         z_recv.at[step, part],
-                        z_peer(depth - step),
+                        z_source(step),
                     )
 
-    for step in range(1, depth):
+    order = sorted(range(own), key=lambda step: abs(2 * (step + 1) - depth))
+    for step in order:
         rows_to_z(step)
-    rows_to_y(0)
-    rows_to_mate(0, 0)
-    from_y(0)
-    from_z(1)
-    from_z(2)
-    from_y(1)
+    rows_to_y(own)
+    rows_to_mate(own, 0)
+    from_y(own)
+    for index, step in enumerate(order):
+        from_z(step)
+        if index >= 1:
+            from_y(order[index - 1])
     for load in loads:
         load.wait()
-    for group, (begin, count) in enumerate(groups):
+    for group in range(len(groups)):
+        if group == len(groups) - 1 and len(groups) == 1:
+            from_y(order[-1])
         first(group)
+        if group == 0 and len(groups) > 1:
+            from_y(order[-1])
         if group >= 1:
             add_y(group - 1)
-        from_z(begin + 3)
-        from_y(begin + 2)
         down(group)
         add_core(group)
-        from_z(begin + 4)
-        from_y(begin + 3)
     add_y(len(groups) - 1)
 
     for part in range(parts):
         columns = slice(part * part_width, (part + 1) * part_width)
-        total = residual_ref[:, columns].astype(jnp.float32) + kept[part, 0, 0]
-        for step in range(1, depth):
+        total = residual_ref[:, columns].astype(jnp.float32) + kept[part, own, 0]
+        for step in range(own):
             landed(z_in.at[part, step], z_recv.at[step, part])
             total = total + z_in[part, step].astype(jnp.float32)
         out_ref[:, columns] = total.astype(out_ref.dtype)
@@ -420,7 +424,7 @@
     block_total = device_total // 2
     typical = max(1, local_rows * TOP // device_total)
     pair_slots = min(local_rows, 4 * typical)
-    if pair_slots == local_rows and device_total % 4 == 0 and device_total <= LANES:
+    if pair_slots == local_rows and device_total % 8 == 0 and device_total <= LANES:
         return dense_mixture(
             residual, norm_gain, expert_ids, route_weights, w_gate, w_up, w_down
         )

time: 36 us -> 36.9 us (1.025)
  Pallas kernels: 34.3 us -> 35.2 us
    pallas_call x1, Pallas kernels: 34.3 us -> 35.2 us  [dense_mixture(): pl.pallas_call(functools.partial(mixture_kernel, depth, groups, parts), o...]
where the time goes in v3:
time: 36.9 us; the launch traced here: 36.7 us
  Pallas kernels  35.2 us (95%)
  local copies, waits for them, and re-layouts  1.47 us (4%)
    pallas_call x1, Pallas kernels, dense_mixture(): pl.pallas_call(functools.partial(mixture_kernel, depth, groups, parts), o...  35.2 us
    unnamed x1, local copies, waits for them, and re-layouts  1.47 us

profile of v3, /device:TPU:0, one launch (start us, length us, event | category | flops | bytes accessed | tf_op | source)
XLA Modules:
  0.0 36.7 jit_solution(16073482070492597640)
XLA Ops:
  0.0 35.2 %shard_map.73 = bf16[16,2048]{1,0:T(8,128)(2,1)} custom-call(bf16[16,2048]{1,0:T(8,128)(2,1)} %residual_hbm.1, bf16[16,128]{1,0:T(8,128)(2,1)} %bitcast.3, s32[8,16]{1,0:T(8,128)} %bitcast.4, f32[8,16]{1,0:T(8,128)} %bitcast.5, bf16[1,2,2048,384]{3,2,1,0:T(8,128)(2,1)} %gate_hbm.1, bf16[1,2,2048,384]{3,2,1,0:T(8,128)(2,1)} %up_hbm.1, ...), custom_call_target="tpu_custom_call" | custom-call | flops 2415919104 | bytes 9437184 | tf_op jit(solution)/shard_map/pallas_call | solution.py:369
  35.2 1.5 %copy.9 = bf16[16,2048]{1,0:T(8,128)(2,1)} copy(bf16[16,2048]{1,0:T(8,128)(2,1)} %shard_map.73) | data formatting | bytes 131072

commit v4 on v2

--- a/solution.py
+++ b/solution.py
@@ -146,8 +146,6 @@
         )
     for load in smalls:
         load.wait()
-    for load in loads:
-        load.start()
 
     widened = residual_ref[...].astype(jnp.float32)
     scaling = lax.rsqrt(jnp.mean(widened * widened, axis=1, keepdims=True) + 1e-06)
@@ -319,6 +317,8 @@
         rows_to_z(step)
     rows_to_y(0)
     rows_to_mate(0, 0)
+    for load in loads:
+        load.start()
     from_y(0)
     from_z(1)
     from_z(2)

time: 36 us -> 36 us (level)
  no operation moved by 1% of the time
where the time goes in v4:
time: 36 us; the launch traced here: 35.8 us
  Pallas kernels  34.3 us (95%)
  local copies, waits for them, and re-layouts  1.47 us (4%)
    pallas_call x1, Pallas kernels, dense_mixture(): pl.pallas_call(functools.partial(mixture_kernel, depth, groups, parts), o...  34.3 us
    unnamed x1, local copies, waits for them, and re-layouts  1.47 us

profile of v4, /device:TPU:0, one launch (start us, length us, event | category | flops | bytes accessed | tf_op | source)
XLA Modules:
  0.0 35.8 jit_solution(14487808021381801005)
XLA Ops:
  0.0 34.3 %shard_map.73 = bf16[16,2048]{1,0:T(8,128)(2,1)} custom-call(bf16[16,2048]{1,0:T(8,128)(2,1)} %residual_hbm.1, bf16[16,128]{1,0:T(8,128)(2,1)} %bitcast.3, s32[8,16]{1,0:T(8,128)} %bitcast.4, f32[8,16]{1,0:T(8,128)} %bitcast.5, bf16[1,2,2048,384]{3,2,1,0:T(8,128)(2,1)} %gate_hbm.1, bf16[1,2,2048,384]{3,2,1,0:T(8,128)(2,1)} %up_hbm.1, ...), custom_call_target="tpu_custom_call" | custom-call | flops 2415919104 | bytes 9437184 | tf_op jit(solution)/shard_map/pallas_call | solution.py:365
  34.3 1.5 %copy.9 = bf16[16,2048]{1,0:T(8,128)(2,1)} copy(bf16[16,2048]{1,0:T(8,128)(2,1)} %shard_map.73) | data formatting | bytes 131072

commit v5 on v4

--- a/solution.py
+++ b/solution.py
@@ -355,7 +355,7 @@
     device_total = lax.axis_size("ep")
     depth = device_total // 4
     groups = [(begin, min(2, depth - begin)) for begin in range(0, depth, 2)]
-    parts = 4
+    parts = 2
     part_width = width // parts
     dma = pltpu.SemaphoreType.DMA
     bf16 = jnp.bfloat16

time: 36 us -> 36 us (level)
  no operation moved by 1% of the time
where the time goes in v5:
time: 36 us; the launch traced here: 35.8 us
  Pallas kernels  34.3 us (95%)
  local copies, waits for them, and re-layouts  1.47 us (4%)
    pallas_call x1, Pallas kernels, dense_mixture(): pl.pallas_call(functools.partial(mixture_kernel, depth, groups, parts), o...  34.3 us
    unnamed x1, local copies, waits for them, and re-layouts  1.47 us

profile of v5, /device:TPU:0, one launch (start us, length us, event | category | flops | bytes accessed | tf_op | source)
XLA Modules:
  0.0 35.8 jit_solution(15148246087856618929)
XLA Ops:
  0.0 34.3 %shard_map.73 = bf16[16,2048]{1,0:T(8,128)(2,1)} custom-call(bf16[16,2048]{1,0:T(8,128)(2,1)} %residual_hbm.1, bf16[16,128]{1,0:T(8,128)(2,1)} %bitcast.3, s32[8,16]{1,0:T(8,128)} %bitcast.4, f32[8,16]{1,0:T(8,128)} %bitcast.5, bf16[1,2,2048,384]{3,2,1,0:T(8,128)(2,1)} %gate_hbm.1, bf16[1,2,2048,384]{3,2,1,0:T(8,128)(2,1)} %up_hbm.1, ...), custom_call_target="tpu_custom_call" | custom-call | flops 2415919104 | bytes 9437184 | tf_op jit(solution)/shard_map/pallas_call | solution.py:365
  34.3 1.5 %copy.9 = bf16[16,2048]{1,0:T(8,128)(2,1)} copy(bf16[16,2048]{1,0:T(8,128)(2,1)} %shard_map.73) | data formatting | bytes 131072
